TPU v7x, 32 devices: a whole 2x2x4 slice. The times are simulated.
32 devices in a mesh: dp: 16 (over z, y, core), tensor: 2 (over x).
Axes of the slice: x: 2, y: 2, z: 4, core: 2. Of those that a mesh axis runs over, the one named last changes fastest.
Arguments:
- hidden_in: bfloat16 [4608, 768], P(('dp', 'tensor')), may hold values from -6 to 6
- lengths: int32 [16, 3], P('dp'), may hold values from 1 to 192, 288 in all within a row
- routes: int32 [4608, 1], P('dp'), may hold values from 0 to 1; in each aligned block of 288 rows (0 to 287, 288 to 575, ...) at most 192 rows name the same one
- gain_attn: float32 [768], replicated, may hold values from 0.5 to 1.5
- wqkv: bfloat16 [768, 3, 768], P('dp', None, 'tensor'), may hold values from -0.21875 to 0.21875
- wo_t: bfloat16 [768, 768], P('dp', 'tensor'), may hold values from -1.75 to 1.75
- bias_table: float32 [32, 12], replicated, may hold values from -4 to 4
- gain_ffn: float32 [768], replicated, may hold values from 0.5 to 1.5
- router: bfloat16 [768, 2], replicated, may hold values from -0.15625 to 0.15625
- w_up: bfloat16 [768, 2, 3072], P('dp', None, 'tensor'), may hold values from -0.21875 to 0.21875
- w_down_t: bfloat16 [768, 2, 3072], P('dp', None, 'tensor'), may hold values from -0.3125 to 0.3125
- cotangent: bfloat16 [4608, 768], P(('dp', 'tensor')), may hold values from -6 to 6
Outputs:
- out_hidden: bfloat16 [4608, 768], P(('dp', 'tensor'))
- grad_input: bfloat16 [4608, 768], P(('dp', 'tensor'))
- grad_gain_attn: float32 [768], replicated
- grad_wqkv: float32 [768, 3, 768], P('dp', None, 'tensor')
- grad_wo: float32 [768, 768], P('dp', 'tensor')
- grad_bias: float32 [32, 12], replicated
- grad_gain_ffn: float32 [768], replicated
- grad_router: float32 [768, 2], replicated
- grad_up: float32 [768, 2, 3072], P('dp', None, 'tensor')
- grad_down: float32 [768, 2, 3072], P('dp', None, 'tensor')
Inputs may be any that keep to these rules, and one draw needn't show every extreme that they name: Each row of lengths holds 3 lengths that sum to 288; the largest is exactly 192. `routes`: in each pack of 288 rows (the rows of one index of dp) at most 192 rows name one expert; in some pack one expert is named by exactly 192 rows.
All inputs are finite; a program needn't handle non-finite values.
Results may differ from a plain program's by a relative error of at most 0.019.
Values may be sent and summed in bfloat16 or wider, within the bound.
A program may use at most 192 MiB of HBM per device.

v0:
```python
import jax
import jax.numpy as jnp
from jax import lax
from jax.sharding import PartitionSpec as P

HD = 64
EXPERTS = 2
BUCKETS = 32
CAP = 192


epsilon = 1e-06
bucket_limits = (12, 16, 23, 32, 46, 64, 91)
highest = lax.Precision.HIGHEST


def normalize(values, gains):
    return values * lax.rsqrt(jnp.mean(values * values, axis=-1, keepdims=True) + epsilon) * gains


def rel_bucket(offsets):
    distance = jnp.abs(offsets)
    beyond = jnp.full(offsets.shape, 8, jnp.int32)
    for limit_value in bucket_limits:
        beyond = beyond + (distance >= limit_value).astype(jnp.int32)
    within = jnp.where(distance < 8, distance, beyond)
    return within + jnp.where(offsets > 0, 16, 0).astype(jnp.int32)


def document_ids(length_row, count):
    bounds = jnp.cumsum(length_row)
    positions = jnp.arange(count, dtype=jnp.int32)
    return jnp.sum((positions[:, None] >= bounds[None, :]).astype(jnp.int32), axis=1)


def slot_ids(route_row):
    onehot = (route_row[:, None] == jnp.arange(EXPERTS, dtype=jnp.int32)[None, :]).astype(jnp.int32)
    before = jnp.cumsum(onehot, axis=0) - onehot
    return route_row * CAP + jnp.sum(before * onehot, axis=1)


def softmax_rows(values):
    shifted = jnp.exp(values - jnp.max(values, axis=-1, keepdims=True))
    return shifted / jnp.sum(shifted, axis=-1, keepdims=True)


def offset_table(row_start, block_rows, key_count):
    span = block_rows + key_count - 1
    offsets = jnp.arange(span, dtype=jnp.int32) - (block_rows - 1) - row_start
    return (rel_bucket(offsets)[:, None] == jnp.arange(BUCKETS, dtype=jnp.int32)[None, :]).astype(
        jnp.float32
    )


def spread_offsets(offset_vals, block_rows, key_count):
    heads_count = offset_vals.shape[0]
    period = block_rows + key_count
    extended = jnp.concatenate([offset_vals, jnp.zeros((heads_count, 1), jnp.float32)], axis=1)
    tiled = jnp.tile(extended, (1, block_rows))
    width = period - 1
    window = tiled[:, block_rows - 1 : block_rows - 1 + block_rows * width]
    return window.reshape(heads_count, block_rows, width)[:, :, :key_count]


def sum_offsets(grad_block, block_rows, key_count):
    heads_count = grad_block.shape[0]
    width = block_rows + key_count - 1
    padded = jnp.pad(grad_block, ((0, 0), (0, 0), (0, width - key_count)))
    flat = padded.reshape(heads_count, block_rows * width)
    flat = jnp.pad(flat, ((0, 0), (block_rows - 1, 1)))
    return jnp.sum(flat.reshape(heads_count, block_rows, width + 1), axis=1)[:, :width]


def block_scores(query_rows, key_rows, row_start, doc_ids, table_cols):
    block_rows = query_rows.shape[0]
    key_count = key_rows.shape[0]
    raw_scores = jnp.einsum(
        "qhd,khd->hqk", query_rows, key_rows, preferred_element_type=jnp.float32
    ) * HD ** (-0.5)
    offset_onehot = offset_table(row_start, block_rows, key_count)
    offset_vals = jnp.dot(offset_onehot, table_cols, precision=highest).T
    bias_rows = spread_offsets(offset_vals, block_rows, key_count)
    same_doc = doc_ids[:, None] == doc_ids[None, :]
    return (jnp.where(same_doc[None], raw_scores + bias_rows, -1e30), offset_onehot)


def shards(
    hidden_in,
    lengths,
    routes,
    gain_attn,
    wqkv,
    wo_t,
    bias_table,
    gain_ffn,
    router,
    w_up,
    w_down_t,
    cotangent,
):
    tensor_rank = lax.axis_index("tensor")
    half_rows = hidden_in.shape[0]
    pack_rows = routes.shape[0]
    model_width = hidden_in.shape[1]
    heads_here = wqkv.shape[2] // HD
    shard_rows = wqkv.shape[0]
    slot_count = EXPERTS * CAP
    query_block = min(pack_rows, 768)
    block_count = pack_rows // query_block
    head_scale = HD ** (-0.5)
    doc_ids = document_ids(lengths[0], pack_rows)
    route_row = routes[:, 0]
    table_cols = lax.dynamic_slice_in_dim(bias_table, tensor_rank * heads_here, heads_here, 1)
    attn_full, out_full = (
        lax.all_gather(wqkv, "dp", axis=0, tiled=True),
        lax.all_gather(wo_t, "dp", axis=0, tiled=True),
    )
    input_rows = hidden_in.astype(jnp.float32)
    norm_one = normalize(input_rows, gain_attn).astype(jnp.bfloat16)
    rows_one = lax.all_gather(norm_one, "tensor", axis=0, tiled=True)
    projected = jnp.dot(
        rows_one, attn_full.reshape(model_width, -1), preferred_element_type=jnp.float32
    )
    projected = projected.astype(jnp.bfloat16).reshape(pack_rows, 3, heads_here, HD)
    queries = projected[:, 0]
    keys_all = projected[:, 1]
    values_all = projected[:, 2]

    def forward_block(block_index):
        row_start = block_index * query_block
        scores, offset_onehot = block_scores(queries, keys_all, row_start, doc_ids, table_cols)
        row_max = jnp.max(scores, axis=-1, keepdims=True)
        exp_scores = jnp.exp(scores - row_max)
        row_total = jnp.sum(exp_scores, axis=-1, keepdims=True)
        probs_low = (exp_scores / row_total).astype(jnp.bfloat16)
        mixed_rows = jnp.einsum(
            "hqk,khd->qhd", probs_low, values_all, preferred_element_type=jnp.float32
        )
        return (
            mixed_rows.astype(jnp.bfloat16).reshape(query_block, -1),
            (row_max + jnp.log(row_total))[..., 0],
        )

    mixed_blocks, log_totals = lax.map(forward_block, jnp.arange(block_count, dtype=jnp.int32))
    mixed = mixed_blocks.reshape(pack_rows, -1)
    attended_part = jnp.einsum("tk,dk->td", mixed, out_full, preferred_element_type=jnp.float32)
    attended = lax.psum_scatter(
        attended_part.astype(jnp.bfloat16), "tensor", scatter_dimension=0, tiled=True
    ).astype(jnp.float32)
    middle = input_rows + attended
    up_full, down_full = (
        lax.all_gather(w_up, "dp", axis=0, tiled=True),
        lax.all_gather(w_down_t, "dp", axis=0, tiled=True),
    )
    norm_two = normalize(middle, gain_ffn).astype(jnp.bfloat16)
    rows_two = lax.all_gather(norm_two, "tensor", axis=0, tiled=True)
    router_probs = softmax_rows(jnp.dot(norm_two, router, preferred_element_type=jnp.float32))
    local_routes = lax.dynamic_slice_in_dim(route_row, tensor_rank * half_rows, half_rows, 0)
    chosen = local_routes[:, None] == jnp.arange(EXPERTS, dtype=jnp.int32)[None, :]
    gate_probs = jnp.sum(jnp.where(chosen, router_probs, 0.0), axis=-1)
    slot_index = slot_ids(route_row)
    dispatch = (slot_index[None, :] == jnp.arange(slot_count, dtype=jnp.int32)[:, None]).astype(
        jnp.bfloat16
    )
    dispatched = jnp.dot(dispatch, rows_two, preferred_element_type=jnp.float32).astype(
        jnp.bfloat16
    )
    dispatched = dispatched.reshape(EXPERTS, CAP, model_width)
    pre_act = jnp.einsum("ecd,def->ecf", dispatched, up_full, preferred_element_type=jnp.float32)
    gelu_value, gelu_back = jax.vjp(jax.nn.gelu, pre_act)
    hidden_act = gelu_value.astype(jnp.bfloat16)
    expert_part = jnp.einsum(
        "ecf,def->ecd", hidden_act, down_full, preferred_element_type=jnp.float32
    )
    token_part = jnp.take(expert_part.reshape(slot_count, model_width), slot_index, axis=0)
    routed = lax.psum_scatter(
        token_part.astype(jnp.bfloat16), "tensor", scatter_dimension=0, tiled=True
    ).astype(jnp.float32)
    out_hidden = (middle + gate_probs[:, None] * routed).astype(jnp.bfloat16)
    grad_top = cotangent.astype(jnp.float32)
    grad_gate = jnp.sum(grad_top * routed, axis=-1)
    scaled_grad = (gate_probs[:, None] * grad_top).astype(jnp.bfloat16)
    grad_tokens = lax.all_gather(scaled_grad, "tensor", axis=0, tiled=True)
    grad_slots = jnp.dot(dispatch, grad_tokens, preferred_element_type=jnp.float32).astype(
        jnp.bfloat16
    )
    grad_slots = grad_slots.reshape(EXPERTS, CAP, model_width)
    grad_act = jnp.einsum("ecd,def->ecf", grad_slots, down_full, preferred_element_type=jnp.float32)
    grad_pre = gelu_back(grad_act)[0].astype(jnp.bfloat16)
    grad_disp = jnp.einsum("ecf,def->ecd", grad_pre, up_full, preferred_element_type=jnp.float32)
    grad_rows_two = jnp.take(grad_disp.reshape(slot_count, model_width), slot_index, axis=0)
    grad_norm_two = lax.psum_scatter(
        grad_rows_two.astype(jnp.bfloat16), "tensor", scatter_dimension=0, tiled=True
    ).astype(jnp.float32)
    picked = jnp.where(chosen, grad_gate[:, None], 0.0)
    grad_logits = router_probs * (picked - jnp.sum(router_probs * picked, axis=-1, keepdims=True))
    router_wide = router.astype(jnp.float32)
    grad_norm_two = grad_norm_two + jnp.dot(grad_logits, router_wide.T, precision=highest)
    grad_router_here = jnp.dot(norm_two.astype(jnp.float32).T, grad_logits, precision=highest)
    norm_two_back = jax.vjp(normalize, middle, gain_ffn)[1]
    grad_middle_norm, grad_gain_ffn_here = norm_two_back(grad_norm_two)
    grad_middle = grad_top + grad_middle_norm
    grad_attended = lax.all_gather(grad_middle.astype(jnp.bfloat16), "tensor", axis=0, tiled=True)
    grad_mixed = jnp.dot(grad_attended, out_full, preferred_element_type=jnp.float32).astype(
        jnp.bfloat16
    )
    grad_mixed = grad_mixed.reshape(pack_rows, heads_here, HD)

    def backward_block(state_tuple, block_index):
        grad_keys, grad_values, grad_table = state_tuple
        row_start = block_index * query_block
        scores, offset_onehot = block_scores(queries, keys_all, row_start, doc_ids, table_cols)
        probs = jnp.exp(scores - log_totals[block_index][..., None])
        probs_low = probs.astype(jnp.bfloat16)
        grad_values = grad_values + jnp.einsum(
            "hqk,qhd->khd", probs_low, grad_mixed, preferred_element_type=jnp.float32
        )
        grad_probs = jnp.einsum(
            "qhd,khd->hqk", grad_mixed, values_all, preferred_element_type=jnp.float32
        )
        grad_scores = probs * (grad_probs - jnp.sum(probs * grad_probs, axis=-1, keepdims=True))
        offset_grads = sum_offsets(grad_scores, query_block, pack_rows)
        grad_table = grad_table + jnp.dot(offset_onehot.T, offset_grads.T, precision=highest)
        scores_low = grad_scores.astype(jnp.bfloat16)
        grad_query_rows = (
            jnp.einsum("hqk,khd->qhd", scores_low, keys_all, preferred_element_type=jnp.float32)
            * head_scale
        )
        grad_keys = (
            grad_keys
            + jnp.einsum("hqk,qhd->khd", scores_low, queries, preferred_element_type=jnp.float32)
            * head_scale
        )
        return ((grad_keys, grad_values, grad_table), grad_query_rows)

    empty_keys = jnp.zeros((pack_rows, heads_here, HD), jnp.float32)
    start_state = (empty_keys, empty_keys, jnp.zeros((BUCKETS, heads_here), jnp.float32))
    final_state, grad_query_blocks = lax.scan(
        backward_block, start_state, jnp.arange(block_count, dtype=jnp.int32)
    )
    grad_keys, grad_values, grad_table = final_state
    grad_queries = grad_query_blocks.reshape(pack_rows, heads_here, HD)
    grad_projected = (
        jnp.stack([grad_queries, grad_keys, grad_values], axis=1)
        .astype(jnp.bfloat16)
        .reshape(pack_rows, -1)
    )
    grad_rows_one = jnp.einsum(
        "tf,df->td",
        grad_projected,
        attn_full.reshape(model_width, -1),
        preferred_element_type=jnp.float32,
    )
    grad_norm_one = lax.psum_scatter(
        grad_rows_one.astype(jnp.bfloat16), "tensor", scatter_dimension=0, tiled=True
    ).astype(jnp.float32)
    norm_one_back = jax.vjp(normalize, input_rows, gain_attn)[1]
    grad_input_norm, grad_gain_attn_here = norm_one_back(grad_norm_one)
    grad_input = (grad_middle + grad_input_norm).astype(jnp.bfloat16)
    column_count = out_full.shape[1]
    proj_rows = jnp.einsum(
        "td,tf->df", rows_one, grad_projected, preferred_element_type=jnp.float32
    )
    proj_rows = proj_rows.reshape(lax.axis_size("dp") * shard_rows, 3, column_count)
    out_rows = jnp.einsum("td,tk->dk", grad_attended, mixed, preferred_element_type=jnp.float32)
    attention_sums = lax.psum_scatter(
        jnp.concatenate([proj_rows, out_rows[:, None, :]], axis=1),
        "dp",
        scatter_dimension=0,
        tiled=True,
    )
    grad_wqkv = attention_sums[:, :3]
    grad_wo = attention_sums[:, 3]
    up_rows = jnp.einsum("ecd,ecf->def", dispatched, grad_pre, preferred_element_type=jnp.float32)
    down_rows = jnp.einsum(
        "ecd,ecf->def", grad_slots, hidden_act, preferred_element_type=jnp.float32
    )
    expert_sums = lax.psum_scatter(
        jnp.stack([up_rows, down_rows], axis=1), "dp", scatter_dimension=0, tiled=True
    )
    grad_up = expert_sums[:, 0]
    grad_down = expert_sums[:, 1]
    table_full = lax.dynamic_update_slice_in_dim(
        jnp.zeros(bias_table.shape, jnp.float32), grad_table, tensor_rank * heads_here, 1
    )
    grad_gain_attn, grad_gain_ffn, grad_bias, grad_router = lax.psum(
        (grad_gain_attn_here, grad_gain_ffn_here, table_full, grad_router_here), ("dp", "tensor")
    )
    return (
        out_hidden,
        grad_input,
        grad_gain_attn,
        grad_wqkv,
        grad_wo,
        grad_bias,
        grad_gain_ffn,
        grad_router,
        grad_up,
        grad_down,
    )


def solution(mesh):
    placed = (
        P(("dp", "tensor"), None),
        P("dp", None),
        P("dp", None),
        P(),
        P("dp", None, "tensor"),
        P("dp", "tensor"),
        P(),
        P(),
        P(),
        P("dp", None, "tensor"),
        P("dp", None, "tensor"),
        P(("dp", "tensor"), None),
    )
    return jax.shard_map(
        shards,
        mesh=mesh,
        in_specs=placed,
        out_specs=(
            P(("dp", "tensor"), None),
            P(("dp", "tensor"), None),
            P(),
            P("dp", None, "tensor"),
            P("dp", "tensor"),
            P(),
            P(),
            P(),
            P("dp", None, "tensor"),
            P("dp", None, "tensor"),
        ),
        check_vma=False,
    )
```

profile of v0, /device:TPU:0, one launch (start us, length us, event | category | flops | bytes accessed | tf_op | source)
XLA Modules:
  0.0 716.4 jit_solution(9055601298565929875)
XLA Ops:
  8.9 2.4 tile.24
  11.3 6.8 tile.25
  18.1 4.9 slice.66
  23.0 9.0 %reshape.252 = f32[6,288,575]{2,1,0:T(8,128)} reshape(f32[6,165600]{1,0:T(8,128)} %slice.66) | data formatting | bytes 7948800 | tf_op jit(solution)/shard_map/while/body/eval_jaxpr/reshape | solution.py:62
  32.5 9.1 %all_gather.24 = bf16[288,768]{1,0:T(8,128)(2,1)S(1)} all-gather(bf16[144,768]{1,0:T(8,128)(2,1)S(1)} %fusion.27), channel_id=1, replica_groups=mesh['dp'=16,'tensor'=2] {'tensor'}, dimensions={0}, use_global_device_ids=true | all-gather | bytes 663552 | tf_op jit(solution)/shard_map/all_gather | solution.py:120
  42.5 23.7 %all_gather.26 = bf16[768,384]{1,0:T(8,128)(2,1)S(1)} all-gather(bf16[48,384]{1,0:T(8,128)(2,1)S(1)} %copy-done.31), channel_id=1, replica_groups=mesh['dp'=16,'tensor'=2] {'dp'}, dimensions={0}, use_global_device_ids=true | all-gather | bytes 626688 | tf_op jit(solution)/shard_map/all_gather | solution.py:116
  66.1 2.8 copy.48
  72.9 2.9 fusion.72
  85.2 6.2 reduce-scatter.6.cloned.1.call-done
  94.3 7.8 %all_gather.27 = bf16[288,768]{1,0:T(8,128)(2,1)S(1)} all-gather(bf16[144,768]{1,0:T(8,128)(2,1)S(1)} %multiply_convert_fusion.1), channel_id=1, replica_groups=mesh['dp'=16,'tensor'=2] {'tensor'}, dimensions={0}, use_global_device_ids=true | all-gather | bytes 663552 | tf_op jit(solution)/shard_map/all_gather | solution.py:156
  102.6 44.9 %all-gather.6.cloned.1.call-done = bf16[768,2,1536]{2,0,1:T(8,128)(2,1)} async-done(((bf16[48,2,1536]{2,0,1:T(8,128)(2,1)}), bf16[768,2,1536]{2,0,1:T(8,128)(2,1)}) %all-gather.6.cloned.1.call-update) | async-done | bytes 4718608 | tf_op jit(solution)/shard_map/all_gather | solution.py:152
  147.4 4.9 fusion.74
  152.3 49.5 %all-gather.8.cloned.1.call-done = bf16[768,2,1536]{2,0,1:T(8,128)(2,1)} async-done(((bf16[48,2,1536]{2,0,1:T(8,128)(2,1)}), bf16[768,2,1536]{2,0,1:T(8,128)(2,1)}) %all-gather.8.cloned.1.call-update) | async-done | bytes 4718608 | tf_op jit(solution)/shard_map/all_gather | solution.py:153
  201.8 4.8 fusion.70
  206.6 2.6 gather_fusion
  212.4 11.1 %reduce-scatter.8.cloned.1.call-done = bf16[144,768]{1,0:T(8,128)(2,1)} async-done(((bf16[288,768]{1,0:T(8,128)(2,1)}), bf16[144,768]{1,0:T(8,128)(2,1)}) %reduce-scatter.8.cloned.1.call-update) | async-done | bytes 221200 | tf_op jit(solution)/shard_map/reduce_scatter | solution.py:176
  225.9 8.1 %all_gather.30 = bf16[288,768]{1,0:T(8,128)(2,1)S(1)} all-gather(bf16[144,768]{1,0:T(8,128)(2,1)S(1)} %fusion.31), channel_id=1, replica_groups=mesh['dp'=16,'tensor'=2] {'tensor'}, dimensions={0}, use_global_device_ids=true | all-gather | bytes 663552 | tf_op jit(solution)/shard_map/all_gather | solution.py:183
  235.2 4.6 fusion.7
  241.6 2.6 gather_fusion.1
  246.3 13.7 %reduce-scatter.10.cloned.1.call-done = bf16[144,768]{1,0:T(8,128)(2,1)} async-done(((bf16[288,768]{1,0:T(8,128)(2,1)}), bf16[144,768]{1,0:T(8,128)(2,1)}) %reduce-scatter.10.cloned.1.call-update) | async-done | bytes 221200 | tf_op jit(solution)/shard_map/reduce_scatter | solution.py:192
  263.1 7.8 %all_gather.31 = bf16[288,768]{1,0:T(8,128)(2,1)S(1)} all-gather(bf16[144,768]{1,0:T(8,128)(2,1)S(1)} %fusion.69), channel_id=1, replica_groups=mesh['dp'=16,'tensor'=2] {'tensor'}, dimensions={0}, use_global_device_ids=true | all-gather | bytes 663552 | tf_op jit(solution)/shard_map/all_gather | solution.py:203
  284.1 2.4 pad_maximum_fusion.1
  287.6 2.8 convolution_bitcast_fusion.1
  292.0 6.9 pad_maximum_fusion
  298.9 28.7 %copy.55 = f32[768,2,2,1536]{3,2,1,0:T(2,128)} copy(f32[768,2,2,1536]{0,3,2,1:T(8,128)} %pad_maximum_fusion) | data formatting | bytes 37748736 | tf_op jit(solution)/shard_map/stack | solution.py:279
  332.3 8.2 %reshape.261 = f32[6,165600]{1,0:T(8,128)} reshape(f32[6,288,575]{2,1,0:T(8,128)} %pad.16) | data formatting | bytes 7948800 | tf_op jit(solution)/shard_map/while/body/eval_jaxpr/reshape | solution.py:69
  340.4 4.9 pad.17
  345.3 6.7 reshape.262
  352.0 2.6 reduce_sum.175
  356.3 40.8 %all-reduce.5 = (f32[768]{0:T(1024)}, f32[32,12]{0,1:T(8,128)}, f32[768]{0:T(1024)}, f32[768,2]{0,1:T(2,128)}) all-reduce(f32[768]{0:T(1024)S(1)} %get-tuple-element.93, f32[32,12]{0,1:T(8,128)S(1)} %dynamic_update_slice.12, f32[768]{0:T(1024)S(1)} %get-tuple-element.91, ...), channel_id=1, replica_groups=mesh['dp'=16,'tensor'=2] {'dp','tensor'}, use_global_device_ids=true, to_apply=%region_22.24 | all-reduce | flops 3456 | bytes 27648 | tf_op jit(solution)/shard_map/psum | solution.py:286
  402.3 304.8 %all-reduce.8.cloned.1.call-done = f32[768,2,2,1536]{3,2,1,0:T(2,128)} async-done(((f32[768,2,2,1536]{3,2,1,0:T(2,128)}), f32[768,2,2,1536]{3,2,1,0:T(2,128)}) %all-reduce.8.cloned.1.call-update) | async-done | bytes 18874384
  707.1 2.3 dynamic-slice_bitcast_fusion
  (173 shorter events, 59.6 us)
Async XLA Ops:
  7.2 58.9 %all-gather.4.cloned.1.call-start = ((), (), s32[]{:S(2)}) async-start(), calls=%async_computation.5 | async-start | bytes 1880064 | tf_op jit(solution)/shard_map/all_gather | solution.py:115
  7.9 83.5 %reduce-scatter.6.cloned.1.call-start = ((), (), s32[]{:S(2)}) async-start(), calls=%async_computation.6 | async-start | bytes 663552 | tf_op jit(solution)/shard_map/reduce_scatter | solution.py:147
  23.0 9.0 %copy-start.36 = (s32[1,3]{1,0:T(1,128)S(1)}, s32[1,3]{1,0:T(1,128)}, u32[]{:S(2)}) copy-start(s32[1,3]{1,0:T(1,128)} %param.15) | copy-start | bytes 40
  23.0 9.2 %copy-start.6 = (bf16[144,768]{1,0:T(8,128)(2,1)S(1)}, bf16[144,768]{1,0:T(8,128)(2,1)}, u32[]{:S(2)}) copy-start(bf16[144,768]{1,0:T(8,128)(2,1)} %param.14) | copy-start | bytes 663556
  23.0 9.3 %copy-start.29 = (f32[768]{0:T(1024)S(1)}, f32[768]{0:T(1024)}, u32[]{:S(2)}) copy-start(f32[768]{0:T(1024)} %param.17) | copy-start | bytes 9220
  23.0 19.4 %copy-start.31 = (bf16[48,384]{1,0:T(8,128)(2,1)S(1)}, bf16[48,384]{1,0:T(8,128)(2,1)}, u32[]{:S(2)}) copy-start(bf16[48,384]{1,0:T(8,128)(2,1)} %param.19) | copy-start | bytes 110596
  41.6 29.0 %copy-start.21 = (bf16[288,768]{1,0:T(8,128)(2,1)}, bf16[288,768]{1,0:T(8,128)(2,1)S(1)}, u32[]{:S(2)}) copy-start(bf16[288,768]{1,0:T(8,128)(2,1)S(1)} %all_gather.24) | copy-start | bytes 1327108
  66.1 12.3 %copy-start.10 = (bf16[768,384]{1,0:T(8,128)(2,1)}, bf16[768,384]{1,0:T(8,128)(2,1)S(1)}, u32[]{:S(2)}) copy-start(bf16[768,384]{1,0:T(8,128)(2,1)S(1)} %all_gather.26) | copy-start | bytes 1769476
  69.0 3.9 copy-start.7
  78.4 5.6 copy-start.32
  78.4 14.1 %copy-start.30 = (f32[768]{0:T(1024)S(1)}, f32[768]{0:T(1024)}, u32[]{:S(2)}) copy-start(f32[768]{0:T(1024)} %param.21) | copy-start | bytes 9220
  80.3 67.1 %all-gather.6.cloned.1.call-start = ((), (), s32[]{:S(2)}) async-start(), calls=%async_computation.7 | async-start | bytes 5013504 | tf_op jit(solution)/shard_map/all_gather | solution.py:152
  82.1 119.7 %all-gather.8.cloned.1.call-start = ((), (), s32[]{:S(2)}) async-start(), calls=%async_computation.8 | async-start | bytes 5013504 | tf_op jit(solution)/shard_map/all_gather | solution.py:153
  83.9 139.6 %reduce-scatter.8.cloned.1.call-start = ((), (), s32[]{:S(2)}) async-start(), calls=%async_computation.9 | async-start | bytes 663552 | tf_op jit(solution)/shard_map/reduce_scatter | solution.py:176
  102.6 49.7 %copy-start.19 = (bf16[384,768]{1,0:T(8,128)(2,1)}, bf16[384,768]{1,0:T(8,128)(2,1)S(1)}, u32[]{:S(2)}) copy-start(bf16[384,768]{1,0:T(8,128)(2,1)S(1)} %convolution_convert_fusion.2) | copy-start | bytes 1769476
  206.6 4.7 copy-start.35
  211.1 48.9 %reduce-scatter.10.cloned.1.call-start = ((), (), s32[]{:S(2)}) async-start(), calls=%async_computation.10 | async-start | bytes 663552 | tf_op jit(solution)/shard_map/reduce_scatter | solution.py:192
  223.5 11.8 %copy-start.4 = (f32[2,192,1536]{2,1,0:T(8,128)S(1)}, f32[2,192,1536]{2,1,0:T(8,128)}, u32[]{:S(2)}) copy-start(f32[2,192,1536]{2,1,0:T(8,128)} %fusion.74) | copy-start | bytes 7077892
  233.9 5.9 slice-start
  235.2 4.7 slice-start.1
  244.2 27.5 %copy-start.11 = (bf16[768,384]{1,0:T(8,128)(2,1)S(1)}, bf16[768,384]{1,0:T(8,128)(2,1)}, u32[]{:S(2)}) copy-start(bf16[768,384]{1,0:T(8,128)(2,1)} %copy-done.10) | copy-start | bytes 1769476
  246.2 108.9 %reduce-scatter.12.cloned.1.call-start = ((), (), s32[]{:S(2)}) async-start(), calls=%async_computation.11 | async-start | bytes 663552 | tf_op jit(solution)/shard_map/reduce_scatter | solution.py:254
  261.7 9.2 %copy-start.23 = (f32[144,768]{1,0:T(8,128)}, f32[144,768]{1,0:T(8,128)S(1)}, u32[]{:S(2)}) copy-start(f32[144,768]{1,0:T(8,128)S(1)} %get-tuple-element.112) | copy-start | bytes 1327108
  280.9 118.2 %reduce-scatter.14.cloned.1.call-start = ((), (), s32[]{:S(2)}) async-start(), calls=%async_computation.12 | async-start | bytes 5013504 | tf_op jit(solution)/shard_map/reduce_scatter | solution.py:266
  286.5 3.9 copy-start.5
  286.5 420.6 %all-reduce.8.cloned.1.call-start = ((), (), s32[]{:S(2)}) async-start(), calls=%async_computation.13 | async-start | bytes 37748736
  287.6 2.9 copy-start.28
  352.0 45.0 %copy-start.15 = (bf16[144,768]{1,0:T(8,128)(2,1)S(1)}, bf16[144,768]{1,0:T(8,128)(2,1)}, u32[]{:S(2)}) copy-start(bf16[144,768]{1,0:T(8,128)(2,1)} %param.25) | copy-start | bytes 663556
  352.0 45.1 %copy-start.16 = (bf16[144,768]{1,0:T(8,128)(2,1)S(1)}, bf16[144,768]{1,0:T(8,128)(2,1)}, u32[]{:S(2)}) copy-start(bf16[144,768]{1,0:T(8,128)(2,1)} %reduce-scatter.6.cloned.1.call-done) | copy-start | bytes 663556
  352.0 45.1 %copy-start.24 = (f32[144,768]{1,0:T(8,128)S(1)}, f32[144,768]{1,0:T(8,128)}, u32[]{:S(2)}) copy-start(f32[144,768]{1,0:T(8,128)} %copy-done.23) | copy-start | bytes 1327108
  352.0 45.1 %copy-start.26 = (bf16[144,768]{1,0:T(8,128)(2,1)S(1)}, bf16[144,768]{1,0:T(8,128)(2,1)}, u32[]{:S(2)}) copy-start(bf16[144,768]{1,0:T(8,128)(2,1)} %reduce-scatter.8.cloned.1.call-done) | copy-start | bytes 663556
  397.0 312.4 %copy-start.1 = (f32[32,12]{0,1:T(8,128)S(1)}, f32[32,12]{0,1:T(8,128)}, u32[]{:S(2)}) copy-start(f32[32,12]{0,1:T(8,128)} %param.20) | copy-start | bytes 4612
  (17 other events, 24.0 us)
Sparse Core Ops, SparseCore 0:
  10.3 43.2 all-gather.3
  80.5 10.9 reduce-scatter.5
  94.0 53.4 all-gather.5
  149.8 51.9 all-gather.7
  211.2 12.1 reduce-scatter.7
  246.3 13.6 reduce-scatter.9
  281.0 13.6 reduce-scatter.11
  298.6 75.8 reduce-scatter.13
  378.8 328.2 all-reduce.7
where the time goes:
time: 725 us; the launch traced here: 716 us
  waiting for transfers between devices  431 us (59%)
  local copies, waits for them, and re-layouts  102 us (14%)
  blocking collectives  97.3 us (13%)
  matrix products  40.2 us (6%)
  other arithmetic  29.1 us (4%)
  between operations  15.7 us (2%)
    unnamed x10, waiting for transfers between devices  306 us
    all_gather x1, waiting for transfers between devices, shards(): lax.all_gather(w_down_t, 'dp', axis=0, tiled=True)  49.5 us
    all_gather x1, waiting for transfers between devices, shards(): lax.all_gather(w_up, 'dp', axis=0, tiled=True)  44.9 us
    psum x1, blocking collectives, shards(): lax.psum((grad_gain_attn_here, grad_gain_ffn_here, table_full, grad_route...  40.8 us
    another operation x1, local copies, waits for them, and re-layouts, shards(): jnp.stack([up_rows, down_rows], axis=1)  28.7 us
    all_gather x1, blocking collectives, shards(): lax.all_gather(wo_t, 'dp', axis=0, tiled=True)  23.7 us
  transfers between devices with their start and end apart: 9, of which 6 were waited for; matrix products, arithmetic and copies ran while one was open for 16% of the time, Pallas kernels for 0%

commit v1 on v0

v1 whole, which is shorter than its diff:
```python
import jax
import jax.numpy as jnp
import numpy as np
from jax import lax
from jax.experimental import pallas as pl
from jax.experimental.pallas import tpu as pltpu
from jax.sharding import PartitionSpec as P

HD = 64
EXPERTS = 2
BUCKETS = 32
CAP = 192

epsilon = 1e-06
bucket_limits = (12, 16, 23, 32, 46, 64, 91)
highest = lax.Precision.HIGHEST
f32 = jnp.float32
bf16 = jnp.bfloat16


def normalize(values, gains):
    return values * lax.rsqrt(jnp.mean(values * values, axis=-1, keepdims=True) + epsilon) * gains


def bucket_onehot(offsets):
    distance = np.abs(offsets)
    beyond = 8 + sum((distance >= limit).astype(np.int32) for limit in bucket_limits)
    buckets = np.where(distance < 8, distance, beyond) + np.where(offsets > 0, 16, 0)
    return jnp.asarray(buckets[:, None] == np.arange(BUCKETS)[None, :], f32)


def dot_nn(a, b):
    return lax.dot_general(a, b, (((1,), (0,)), ((), ())), preferred_element_type=f32)


def dot_nt(a, b):
    return lax.dot_general(a, b, (((1,), (1,)), ((), ())), preferred_element_type=f32)


def dot_tn(a, b):
    return lax.dot_general(a, b, (((0,), (0,)), ((), ())), preferred_element_type=f32)


def head_probs(q, k, v_ref, same, h, rows, wide):
    raw = dot_nt(q, k) * HD ** (-0.5)
    spread = jnp.broadcast_to(v_ref[h : h + 1, :], (rows, wide))
    bias = pltpu.roll(spread, 0, 1, stride=1, stride_axis=0)[:, :rows]
    scores = jnp.where(same, raw + bias, -1e30)
    shifted = jnp.exp(scores - jnp.max(scores, axis=-1, keepdims=True))
    return shifted / jnp.sum(shifted, axis=-1, keepdims=True)


def forward_kernel(heads, rows, wide, qkv_ref, v_ref, dc_ref, dr_ref, out_ref):
    same = dc_ref[...] == dr_ref[...]
    width = heads * HD
    for h in range(heads):
        cut = slice(h * HD, (h + 1) * HD)
        q = qkv_ref[:, h * HD : (h + 1) * HD]
        k = qkv_ref[:, width + h * HD : width + (h + 1) * HD]
        v = qkv_ref[:, 2 * width + h * HD : 2 * width + (h + 1) * HD]
        probs = head_probs(q, k, v_ref, same, h, rows, wide)
        out_ref[:, cut] = dot_nn(probs.astype(bf16), v).astype(bf16)


def backward_kernel(heads, rows, wide, qkv_ref, gm_ref, v_ref, dc_ref, dr_ref, gp_ref, diag_ref):
    same = dc_ref[...] == dr_ref[...]
    width = heads * HD
    flip = (
        lax.broadcasted_iota(jnp.int32, (rows, rows), 0)
        + lax.broadcasted_iota(jnp.int32, (rows, rows), 1)
        == rows - 1
    ).astype(f32).astype(bf16)
    diag_ref[...] = jnp.zeros_like(diag_ref)
    for h in range(heads):
        q = qkv_ref[:, h * HD : (h + 1) * HD]
        k = qkv_ref[:, width + h * HD : width + (h + 1) * HD]
        v = qkv_ref[:, 2 * width + h * HD : 2 * width + (h + 1) * HD]
        g = gm_ref[:, h * HD : (h + 1) * HD]
        probs = head_probs(q, k, v_ref, same, h, rows, wide)
        gv = dot_tn(probs.astype(bf16), g)
        gprobs = dot_nt(g, v)
        ds = probs * (gprobs - jnp.sum(probs * gprobs, axis=-1, keepdims=True))
        low = ds.astype(bf16)
        gq = dot_nn(low, k) * HD ** (-0.5)
        gk = dot_tn(low, q) * HD ** (-0.5)
        gp_ref[:, h * HD : (h + 1) * HD] = gq.astype(bf16)
        gp_ref[:, width + h * HD : width + (h + 1) * HD] = gk.astype(bf16)
        gp_ref[:, 2 * width + h * HD : 2 * width + (h + 1) * HD] = gv.astype(bf16)
        turned = dot_nn(flip, low)
        padded = jnp.concatenate([turned, jnp.zeros((rows, wide - rows), f32)], axis=1)
        rolled = pltpu.roll(padded, 0, 1, stride=1, stride_axis=0)
        diag_ref[h : h + 1, :] = jnp.sum(rolled, axis=0, keepdims=True)


def call_kernel(body, outs, flops, *operands):
    return pl.pallas_call(
        body,
        out_shape=outs,
        in_specs=[pl.BlockSpec(memory_space=pltpu.VMEM)] * len(operands),
        out_specs=jax.tree.map(lambda _: pl.BlockSpec(memory_space=pltpu.VMEM), outs),
        compiler_params=pltpu.CompilerParams(vmem_limit_bytes=40 * 2**20),
        cost_estimate=pl.CostEstimate(flops=flops, bytes_accessed=2**21, transcendentals=2**20),
    )(*operands)


def make_links(dp):
    def by(mask):
        return [(i, i ^ mask) for i in range(dp)]

    ring = [(i, (i + 4) % dp) for i in range(dp)]

    def move(x, perm):
        return lax.ppermute(x, "dp", perm)

    def gather(own):
        if dp != 16:
            full = lax.all_gather(own, "dp", axis=0, tiled=True)
            return full[: full.shape[0] // 2], full[full.shape[0] // 2 :]
        held, sides = [own], [move(own, by(2))]
        for _ in range(3):
            held.append(move(held[-1], ring))
            sides.append(move(held[-1], by(2)))
        near = jnp.concatenate(held + sides, axis=0)
        return near, move(near, by(1))

    def add(a, b):
        return a.astype(f32) + b.astype(f32)

    def scatter(keep, send):
        if dp != 16:
            return lax.psum_scatter(
                jnp.concatenate([keep, send], axis=0), "dp", scatter_dimension=0, tiled=True
            ).astype(f32)
        got = move(send.astype(bf16), by(1))
        half = keep.shape[0] // 2
        far = add(keep[half:], got[half:]).astype(bf16)
        near = add(keep[:half], got[:half])
        got = move(far, by(2))
        near = add(near, got)
        part = half // 4
        chunk = near[part : 2 * part].astype(bf16)
        for step in range(3):
            got = move(chunk, ring)
            at = (step + 2) % 4
            total = add(near[at * part : (at + 1) * part], got)
            chunk = total.astype(bf16)
        return total

    def total(x):
        if dp != 16:
            return lax.psum(x, ("dp", "tensor"))
        x = x + lax.ppermute(x, "tensor", [(0, 1), (1, 0)])
        for mask in (1, 2, 4, 8):
            x = x + move(x, by(mask))
        return x

    return gather, scatter, total


def shards(
    hidden_in,
    lengths,
    routes,
    gain_attn,
    wqkv,
    wo_t,
    bias_table,
    gain_ffn,
    router,
    w_up,
    w_down_t,
    cotangent,
):
    dp = lax.axis_size("dp")
    gather, scatter, total = make_links(dp)
    rank = lax.axis_index("tensor")
    half_rows = hidden_in.shape[0]
    rows = routes.shape[0]
    width = hidden_in.shape[1]
    mid = width // 2
    cols = wqkv.shape[2]
    heads = cols // HD
    hidden = w_up.shape[2]
    depth = wqkv.shape[0]
    slot_count = EXPERTS * CAP
    wide = 128 * (-(-2 * rows // 128))

    def swap(x):
        return lax.ppermute(x, "tensor", [(0, 1), (1, 0)])

    def whole_rows(own):
        other = swap(own)
        return jnp.where(
            rank == 0, jnp.concatenate([own, other]), jnp.concatenate([other, own])
        )

    def own_rows(x, who):
        return lax.dynamic_slice_in_dim(x, who * half_rows, half_rows, 0)

    attn_own = jnp.concatenate([wqkv.reshape(depth, 3 * cols), wo_t], axis=1)
    attn_w = gather(attn_own)
    up_w = gather(w_up.reshape(depth, EXPERTS * hidden))
    down_w = gather(w_down_t.reshape(depth, EXPERTS * hidden))

    place = jnp.arange(width, dtype=jnp.int32)
    if dp == 16:
        me = lax.axis_index("dp")
        z, y, core = me // 4, (me // 2) % 2, me % 2
        from_core = (core + place // mid) % 2
        from_y = (y + (place // (mid // 2)) % 2) % 2
        from_z = (z + 4 - (place // depth) % 4) % 4
        origin = (from_z * 4 + from_y * 2 + from_core) * depth + place % depth
    else:
        origin = place
    to_here = (place[:, None] == origin[None, :]).astype(bf16)

    hid = dot_nn(whole_rows(hidden_in), to_here)
    cot = dot_nn(whole_rows(cotangent), to_here)
    vectors = jnp.concatenate(
        [gain_attn[None], gain_ffn[None], router.astype(f32).T], axis=0
    )
    vectors = jnp.dot(vectors, to_here.astype(f32), precision=highest)
    gain_one, gain_two, router_here = vectors[0], vectors[1], vectors[2:].astype(bf16)

    positions = jnp.arange(rows, dtype=jnp.int32)
    first, second = lengths[0, 0], lengths[0, 0] + lengths[0, 1]
    docs = (
        (positions >= first).astype(jnp.int32)
        + (positions >= second).astype(jnp.int32)
        + (positions >= second + lengths[0, 2]).astype(jnp.int32)
    )
    doc_col, doc_row = docs[:, None], docs[None, :]
    table_cols = lax.dynamic_slice_in_dim(bias_table, rank * heads, heads, 1)
    turn = np.arange(wide)
    spread = bucket_onehot(np.where(turn < rows, turn, turn - wide))
    offset_vals = jnp.dot(table_cols.T, spread.T, precision=highest)

    norm_one = normalize(hid, gain_one).astype(bf16)
    projected = dot_nn(norm_one[:, :mid], attn_w[0][:, : 3 * cols])
    projected = projected + dot_nn(norm_one[:, mid:], attn_w[1][:, : 3 * cols])
    projected = projected.astype(bf16)
    flops = 2 * heads * rows * rows * HD
    mixed = call_kernel(
        lambda *refs: forward_kernel(heads, rows, wide, *refs),
        jax.ShapeDtypeStruct((rows, cols), bf16),
        2 * flops,
        projected,
        offset_vals,
        doc_col,
        doc_row,
    )
    out_w = [w[:, 3 * cols :] for w in attn_w]
    attended_part = jnp.concatenate([dot_nt(mixed, w) for w in out_w], axis=1).astype(bf16)
    middle = hid + (attended_part.astype(f32) + swap(attended_part).astype(f32))

    norm_two = normalize(middle, gain_two).astype(bf16)
    logits = dot_nt(norm_two, router_here)
    shifted = jnp.exp(logits - jnp.max(logits, axis=-1, keepdims=True))
    router_probs = shifted / jnp.sum(shifted, axis=-1, keepdims=True)
    chosen = routes == jnp.arange(EXPERTS, dtype=jnp.int32)[None, :]
    gate = jnp.sum(jnp.where(chosen, router_probs, 0.0), axis=-1, keepdims=True)
    earlier = (positions[:, None] < positions[None, :]) & (routes == routes[:, 0][None, :])
    slot_index = routes[:, 0] * CAP + jnp.sum(earlier.astype(jnp.int32), axis=0)
    dispatch = (
        slot_index[None, :] == jnp.arange(slot_count, dtype=jnp.int32)[:, None]
    ).astype(bf16)

    def expert_cut(pair, e):
        return [w[:, e * hidden : (e + 1) * hidden] for w in pair]

    up_e = [expert_cut(up_w, e) for e in range(EXPERTS)]
    down_e = [expert_cut(down_w, e) for e in range(EXPERTS)]

    def into(x, pair):
        return dot_nn(x[:, :mid], pair[0]) + dot_nn(x[:, mid:], pair[1])

    def out_of(x, pair):
        return jnp.concatenate([dot_nt(x, w) for w in pair], axis=1)

    def to_tokens(parts):
        return dot_tn(dispatch, jnp.concatenate(parts, axis=0)).astype(bf16)

    dispatched = dot_nn(dispatch, norm_two).astype(bf16)
    scaled_grad = (gate * cot).astype(bf16)
    grad_slots = dot_nn(dispatch, scaled_grad).astype(bf16)
    disp_e = [dispatched[e * CAP : (e + 1) * CAP] for e in range(EXPERTS)]
    slots_e = [grad_slots[e * CAP : (e + 1) * CAP] for e in range(EXPERTS)]

    hidden_act, grad_pre = [], []
    for e in range(EXPERTS):
        value, back = jax.vjp(jax.nn.gelu, into(disp_e[e], up_e[e]))
        hidden_act.append(value.astype(bf16))
        grad_pre.append(back(into(slots_e[e], down_e[e]))[0].astype(bf16))
    grad_rows = to_tokens([out_of(grad_pre[e], up_e[e]).astype(bf16) for e in range(EXPERTS)])
    token_part = to_tokens([out_of(hidden_act[e], down_e[e]).astype(bf16) for e in range(EXPERTS)])
    routed = token_part.astype(f32) + swap(token_part).astype(f32)
    grad_rows = grad_rows.astype(f32) + swap(grad_rows).astype(f32)

    def weight_grad(left, right):
        return scatter(
            dot_tn(left[:, :mid], right).astype(bf16), dot_tn(left[:, mid:], right).astype(bf16)
        )

    grad_up = jnp.stack([weight_grad(disp_e[e], grad_pre[e]) for e in range(EXPERTS)], axis=1)
    grad_down = jnp.stack([weight_grad(slots_e[e], hidden_act[e]) for e in range(EXPERTS)], axis=1)

    out_rows = own_rows(middle + gate * routed, rank).astype(bf16)
    out_hidden = dot_nt(out_rows, to_here).astype(bf16)
    grad_gate = jnp.sum(cot * routed, axis=-1, keepdims=True)
    picked = jnp.where(chosen, grad_gate, 0.0)
    grad_logits = router_probs * (picked - gate * grad_gate)
    router_wide = router_here.astype(f32)
    grad_norm_two = grad_rows + sum(
        grad_logits[:, e : e + 1] * router_wide[e : e + 1] for e in range(EXPERTS)
    )
    grad_router_here = jnp.stack(
        [
            jnp.sum(norm_two.astype(f32) * grad_logits[:, e : e + 1], axis=0)
            for e in range(EXPERTS)
        ]
    )
    grad_middle_norm, grad_gain_ffn = jax.vjp(normalize, middle, gain_two)[1](grad_norm_two)
    grad_middle = cot + grad_middle_norm

    grad_attended = grad_middle.astype(bf16)
    grad_mixed = into(grad_attended, out_w).astype(bf16)
    grad_projected, diagonals = call_kernel(
        lambda *refs: backward_kernel(heads, rows, wide, *refs),
        (
            jax.ShapeDtypeStruct((rows, 3 * cols), bf16),
            jax.ShapeDtypeStruct((8, wide), f32),
        ),
        6 * flops,
        projected,
        grad_mixed,
        offset_vals,
        doc_col,
        doc_row,
    )
    grad_rows_one = out_of(grad_projected, [w[:, : 3 * cols] for w in attn_w]).astype(bf16)
    arrived = swap(own_rows(grad_rows_one, 1 - rank))
    grad_norm_one = own_rows(grad_rows_one, rank).astype(f32) + arrived.astype(f32)
    grad_input_norm, grad_gain_attn = jax.vjp(normalize, own_rows(hid, rank), gain_one)[1](
        grad_norm_one
    )
    grad_input = (own_rows(grad_middle, rank) + grad_input_norm).astype(bf16)
    grad_input = dot_nt(grad_input, to_here).astype(bf16)

    attention_sums = scatter(
        *[
            jnp.concatenate(
                [dot_tn(norm_one[:, cut], grad_projected), dot_tn(grad_attended[:, cut], mixed)],
                axis=1,
            ).astype(bf16)
            for cut in (slice(0, mid), slice(mid, width))
        ]
    )
    grad_wqkv = attention_sums[:, : 3 * cols].reshape(depth, 3, cols)
    grad_wo = attention_sums[:, 3 * cols :]

    small = jnp.concatenate(
        [grad_gain_attn[None], 0.5 * grad_gain_ffn[None], 0.5 * grad_router_here], axis=0
    )
    small = lax.dot_general(
        small, to_here.astype(f32), (((1,), (1,)), ((), ())), precision=highest
    )
    by_bucket = bucket_onehot(turn - (rows - 1))
    grad_table = jnp.dot(by_bucket.T, diagonals[:heads].T, precision=highest)
    table_full = lax.dynamic_update_slice_in_dim(
        jnp.zeros(bias_table.shape, f32), grad_table, rank * heads, 1
    )
    flat = table_full.reshape(1, -1)
    flat = jnp.pad(flat, ((0, 0), (0, width - flat.shape[1])))
    sums = total(jnp.concatenate([small, flat], axis=0))
    grad_bias = sums[4, : table_full.size].reshape(bias_table.shape)
    return (
        out_hidden,
        grad_input,
        sums[0],
        grad_wqkv,
        grad_wo,
        grad_bias,
        sums[1],
        sums[2:4].T,
        grad_up,
        grad_down,
    )


def solution(mesh):
    placed = (
        P(("dp", "tensor"), None),
        P("dp", None),
        P("dp", None),
        P(),
        P("dp", None, "tensor"),
        P("dp", "tensor"),
        P(),
        P(),
        P(),
        P("dp", None, "tensor"),
        P("dp", None, "tensor"),
        P(("dp", "tensor"), None),
    )
    return jax.shard_map(
        shards,
        mesh=mesh,
        in_specs=placed,
        out_specs=(
            P(("dp", "tensor"), None),
            P(("dp", "tensor"), None),
            P(),
            P("dp", None, "tensor"),
            P("dp", "tensor"),
            P(),
            P(),
            P(),
            P("dp", None, "tensor"),
            P("dp", None, "tensor"),
        ),
        check_vma=False,
    )
```

time: 725 us -> 345 us (0.48)
  waiting for transfers between devices: 431 us -> 207 us
  blocking collectives: 97.3 us -> 0 us
  local copies, waits for them, and re-layouts: 102 us -> 17.1 us
  starting transfers between devices: 0.62 us -> 40.3 us
  between operations: 15.7 us -> 3.97 us
  Pallas kernels: 0 us -> 11.3 us
  other arithmetic: 29.1 us -> 20.7 us
    unnamed x10 -> x0, waiting for transfers between devices: 306 us -> none
    ppermute x0 -> x60, waiting for transfers between devices: none -> 207 us  [the longest x53 169 us: move(): return lax.ppermute(x, 'dp', perm)]
    all_gather x3 -> x0, waiting for transfers between devices: 94.4 us -> none  [the longest x1 49.5 us: shards(): lax.all_gather(w_down_t, 'dp', axis=0, tiled=True)]
    all_gather x5 -> x0, blocking collectives: 56.5 us -> none  [the longest x1 23.7 us: shards(): lax.all_gather(wo_t, 'dp', axis=0, tiled=True)]
    psum x1 -> x0, blocking collectives: 40.8 us -> none  [shards(): lax.psum((grad_gain_attn_here, grad_gain_ffn_here, table_full, grad_route...]
    ppermute x0 -> x60, starting transfers between devices: none -> 40.3 us  [the longest x53 32.1 us: move(): return lax.ppermute(x, 'dp', perm)]
    another operation x5 -> x3, local copies, waits for them, and re-layouts: 38.1 us -> 0.11 us  [the longest x1 0.1 us: shards(): grad_bias = sums[4, :table_full.size].reshape(bias_table.shape)]
    reduce_scatter x5 -> x0, waiting for transfers between devices: 31.1 us -> none  [the longest x1 13.7 us: shards(): lax.psum_scatter(grad_rows_two.astype(jnp.bfloat16), 'tensor', scatter_di...]
  transfers between devices with their start and end apart: 9 -> 60, of which waited for: 6 -> 37; matrix products, arithmetic and copies ran while one was open for 16% -> 16% of each run, Pallas kernels for 0% -> 3%
where the time goes in v1:
time: 345 us; the launch traced here: 340 us
  waiting for transfers between devices  207 us (60%)
  starting transfers between devices  40.3 us (12%)
  matrix products  39.9 us (12%)
  other arithmetic  20.7 us (6%)
  local copies, waits for them, and re-layouts  17.1 us (5%)
  Pallas kernels  11.3 us (3%)
  between operations  3.97 us (1%)
    ppermute x53, waiting for transfers between devices, move(): return lax.ppermute(x, 'dp', perm)  169 us
    ppermute x6, waiting for transfers between devices, swap(): return lax.ppermute(x, 'tensor', [(0, 1), (1, 0)])  35.5 us
    ppermute x53, starting transfers between devices, move(): return lax.ppermute(x, 'dp', perm)  32.1 us
    dot_general x14, matrix products, dot_tn(): lax.dot_general(a, b, (((0,), (0,)), ((), ())), preferred_element_type=f32)  16.4 us
    pallas_call x2, Pallas kernels, call_kernel(): pl.pallas_call(body, out_shape=outs, in_specs=[pl.BlockSpec(memory_space=...  11.3 us
    unnamed x82, local copies, waits for them, and re-layouts  10.8 us
    dot_general x16, matrix products, dot_nn(): lax.dot_general(a, b, (((1,), (0,)), ((), ())), preferred_element_type=f32)  10.3 us
    dot_general x15, matrix products, dot_nt(): lax.dot_general(a, b, (((1,), (1,)), ((), ())), preferred_element_type=f32)  10.1 us
  transfers between devices with their start and end apart: 60, of which 37 were waited for; matrix products, arithmetic and copies ran while one was open for 16% of the time, Pallas kernels for 3%

profile of v1, /device:TPU:0, one launch (start us, length us, event | category | flops | bytes accessed | tf_op | source)
XLA Modules:
  0.0 339.8 jit_solution(15039076373013217579)
XLA Ops:
  21.7 4.4 %collective-permute-done = bf16[144,768]{1,0:T(8,128)(2,1)S(1)} collective-permute-done((bf16[144,768]{1,0:T(8,128)(2,1)S(1)}, bf16[144,768]{1,0:T(8,128)(2,1)S(1)}, u32[]{:S(2)}, u32[]{:S(2)}) %collective-permute-start) | collective-permute-done | bytes 221216 | tf_op jit(solution)/shard_map/ppermute | solution.py:189
  30.3 5.6 %collective-permute-done.2 = bf16[48,1536]{1,0:T(8,128)(2,1)S(1)} collective-permute-done((bf16[48,1536]{1,0:T(8,128)(2,1)S(1)}, bf16[48,1536]{1,0:T(8,128)(2,1)S(1)}, u32[]{:S(2)}, u32[]{:S(2)}) %collective-permute-start.2) | collective-permute-done | bytes 147488 | tf_op jit(solution)/shard_map/ppermute | solution.py:113
  38.4 5.9 %collective-permute-done.3 = bf16[48,1536]{1,0:T(8,128)(2,1)S(1)} collective-permute-done((bf16[48,1536]{1,0:T(8,128)(2,1)S(1)}, bf16[48,1536]{1,0:T(8,128)(2,1)S(1)}, u32[]{:S(2)}, u32[]{:S(2)}) %collective-permute-start.3) | collective-permute-done | bytes 147488 | tf_op jit(solution)/shard_map/ppermute | solution.py:113
  47.4 3.1 collective-permute-done.5
  52.6 5.0 %collective-permute-done.7 = bf16[48,1536]{1,0:T(8,128)(2,1)S(1)} collective-permute-done((bf16[48,1536]{1,0:T(8,128)(2,1)S(1)}, bf16[48,1536]{1,0:T(8,128)(2,1)S(1)}, u32[]{:S(2)}, u32[]{:S(2)}) %collective-permute-start.7) | collective-permute-done | bytes 147488 | tf_op jit(solution)/shard_map/ppermute | solution.py:113
  58.2 3.7 %collective-permute-done.11 = bf16[48,3072]{1,0:T(8,128)(2,1)S(1)} collective-permute-done((bf16[48,3072]{1,0:T(8,128)(2,1)}, bf16[48,3072]{1,0:T(8,128)(2,1)S(1)}, u32[]{:S(2)}, u32[]{:S(2)}) %collective-permute-start.11) | collective-permute-done | bytes 294944 | tf_op jit(solution)/shard_map/ppermute | solution.py:113
  62.0 10.5 %collective-permute-done.19 = bf16[48,3072]{1,0:T(8,128)(2,1)S(1)} collective-permute-done((bf16[48,3072]{1,0:T(8,128)(2,1)}, bf16[48,3072]{1,0:T(8,128)(2,1)S(1)}, u32[]{:S(2)}, u32[]{:S(2)}) %collective-permute-start.19) | collective-permute-done | bytes 294944 | tf_op jit(solution)/shard_map/ppermute | solution.py:113
  72.4 8.5 %collective-permute-done.12 = bf16[48,3072]{1,0:T(8,128)(2,1)S(1)} collective-permute-done((bf16[48,3072]{1,0:T(8,128)(2,1)S(1)}, bf16[48,3072]{1,0:T(8,128)(2,1)S(1)}, u32[]{:S(2)}, u32[]{:S(2)}) %collective-permute-start.12) | collective-permute-done | bytes 294944 | tf_op jit(solution)/shard_map/ppermute | solution.py:113
  84.2 10.0 %collective-permute-done.15 = bf16[48,3072]{1,0:T(8,128)(2,1)S(1)} collective-permute-done((bf16[48,3072]{1,0:T(8,128)(2,1)S(1)}, bf16[48,3072]{1,0:T(8,128)(2,1)S(1)}, u32[]{:S(2)}, u32[]{:S(2)}) %collective-permute-start.15) | collective-permute-done | bytes 294944 | tf_op jit(solution)/shard_map/ppermute | solution.py:113
  94.4 9.3 %collective-permute-done.20 = bf16[48,3072]{1,0:T(8,128)(2,1)S(1)} collective-permute-done((bf16[48,3072]{1,0:T(8,128)(2,1)S(1)}, bf16[48,3072]{1,0:T(8,128)(2,1)S(1)}, u32[]{:S(2)}, u32[]{:S(2)}) %collective-permute-start.20) | collective-permute-done | bytes 294944 | tf_op jit(solution)/shard_map/ppermute | solution.py:113
  106.8 12.9 %collective-permute-done.16 = bf16[48,3072]{1,0:T(8,128)(2,1)S(1)} collective-permute-done((bf16[48,3072]{1,0:T(8,128)(2,1)S(1)}, bf16[48,3072]{1,0:T(8,128)(2,1)S(1)}, u32[]{:S(2)}, u32[]{:S(2)}) %collective-permute-start.16) | collective-permute-done | bytes 294944 | tf_op jit(solution)/shard_map/ppermute | solution.py:113
  120.9 4.4 %shard_map.213 = bf16[288,384]{1,0:T(8,128)(2,1)S(1)} custom-call(bf16[288,1152]{1,0:T(8,128)(2,1)S(1)} %fusion.refs_0_, f32[6,640]{1,0:T(8,128)S(1)} %fusion.180.refs_1_.refs_2_, s32[288,1]{1,0:T(8,128)S(1)} %convert_add_fusion.7.refs_2_.refs_3_, s32[1,288]{1,0:T(1,128)S(1)} %fusion.189.refs_3_.refs_4_), custom_call_target="tpu_custom_call" | custom-call | flops 127401984 | bytes 2097152 | tf_op jit(solution)/shard_map/pallas_call | solution.py:96
  127.4 11.2 %collective-permute-done.9 = bf16[288,768]{1,0:T(8,128)(2,1)S(1)} collective-permute-done((bf16[288,768]{1,0:T(8,128)(2,1)S(1)}, bf16[288,768]{1,0:T(8,128)(2,1)S(1)}, u32[]{:S(2)}, u32[]{:S(2)}) %collective-permute-start.9) | collective-permute-done | bytes 442400 | tf_op jit(solution)/shard_map/ppermute | solution.py:189
  146.0 10.4 %collective-permute-done.26 = bf16[288,768]{1,0:T(8,128)(2,1)S(1)} collective-permute-done((bf16[288,768]{1,0:T(8,128)(2,1)S(1)}, bf16[288,768]{1,0:T(8,128)(2,1)S(1)}, u32[]{:S(2)}, u32[]{:S(2)}) %collective-permute-start.26) | collective-permute-done | bytes 442400 | tf_op jit(solution)/shard_map/ppermute | solution.py:189
  180.1 6.0 %collective-permute-done.28 = bf16[288,768]{1,0:T(8,128)(2,1)S(1)} collective-permute-done((bf16[288,768]{1,0:T(8,128)(2,1)S(1)}, bf16[288,768]{1,0:T(8,128)(2,1)S(1)}, u32[]{:S(2)}, u32[]{:S(2)}) %collective-permute-start.28) | collective-permute-done | bytes 442400 | tf_op jit(solution)/shard_map/ppermute | solution.py:189
  188.8 6.9 %shard_map.214 = (bf16[288,1152]{1,0:T(8,128)(2,1)S(1)}, f32[8,640]{1,0:T(8,128)S(1)}) custom-call(bf16[288,1152]{1,0:T(8,128)(2,1)S(1)} %fusion.refs_0_, bf16[288,384]{1,0:T(8,128)(2,1)S(1)} %fusion.9.refs_1_, f32[6,640]{1,0:T(8,128)S(1)} %fusion.180.refs_1_.refs_2_, s32[288,1]{1,0:T(8,128)S(1)} %convert_add_fusion.7.refs_2_.refs_3_, ...), custom_call_target="tpu_custom_call" | custom-call | flops 382205952 | bytes 2097152 | tf_op jit(solution)/shard_map/pallas_call | solution.py:96
  202.0 3.4 %collective-permute-done.29 = bf16[144,768]{1,0:T(8,128)(2,1)} collective-permute-done((bf16[144,768]{1,0:T(8,128)(2,1)}, bf16[144,768]{1,0:T(8,128)(2,1)}, u32[]{:S(2)}, u32[]{:S(2)}) %collective-permute-start.29) | collective-permute-done | bytes 221216 | tf_op jit(solution)/shard_map/ppermute | solution.py:189
  216.8 3.8 %collective-permute-done.33 = f32[5,768]{1,0:T(8,128)S(1)} collective-permute-done((f32[5,768]{1,0:T(8,128)S(1)}, f32[5,768]{1,0:T(8,128)S(1)}, u32[]{:S(2)}, u32[]{:S(2)}) %collective-permute-start.33) | collective-permute-done | bytes 15392 | tf_op jit(solution)/shard_map/ppermute | solution.py:113
  238.8 6.1 %collective-permute-done.46 = bf16[192,1536]{1,0:T(8,128)(2,1)S(1)} collective-permute-done((bf16[192,1536]{1,0:T(8,128)(2,1)S(1)}, bf16[192,1536]{1,0:T(8,128)(2,1)S(1)}, u32[]{:S(2)}, u32[]{:S(2)}) %collective-permute-start.46) | collective-permute-done | bytes 589856 | tf_op jit(solution)/shard_map/ppermute | solution.py:113
  246.3 11.3 %collective-permute-done.41 = bf16[192,1536]{1,0:T(8,128)(2,1)S(1)} collective-permute-done((bf16[192,1536]{1,0:T(8,128)(2,1)S(1)}, bf16[192,1536]{1,0:T(8,128)(2,1)S(1)}, u32[]{:S(2)}, u32[]{:S(2)}) %collective-permute-start.41) | collective-permute-done | bytes 589856 | tf_op jit(solution)/shard_map/ppermute | solution.py:113
  258.9 11.3 %collective-permute-done.56 = bf16[192,1536]{1,0:T(8,128)(2,1)S(1)} collective-permute-done((bf16[192,1536]{1,0:T(8,128)(2,1)S(1)}, bf16[192,1536]{1,0:T(8,128)(2,1)S(1)}, u32[]{:S(2)}, u32[]{:S(2)}) %collective-permute-start.56) | collective-permute-done | bytes 589856 | tf_op jit(solution)/shard_map/ppermute | solution.py:113
  271.6 11.3 %collective-permute-done.51 = bf16[192,1536]{1,0:T(8,128)(2,1)S(1)} collective-permute-done((bf16[192,1536]{1,0:T(8,128)(2,1)S(1)}, bf16[192,1536]{1,0:T(8,128)(2,1)S(1)}, u32[]{:S(2)}, u32[]{:S(2)}) %collective-permute-start.51) | collective-permute-done | bytes 589856 | tf_op jit(solution)/shard_map/ppermute | solution.py:113
  285.6 3.8 %collective-permute-start.58 = (bf16[48,1536]{1,0:T(8,128)(2,1)S(1)}, bf16[48,1536]{1,0:T(8,128)(2,1)S(1)}, u32[]{:S(2)}, u32[]{:S(2)}) collective-permute-start(bf16[48,1536]{1,0:T(8,128)(2,1)S(1)} %fusion.91), channel_id=1, source_target_pairs={{0,8},{2,10},{4,12},{6,14},{8,16},{10,18},{12,20},{14,22},{16,24},... | collective-permute-start | bytes 442376 | tf_op jit(solution)/shard_map/ppermute | solution.py:113
  289.4 3.4 collective-permute-done.52
  292.9 3.1 collective-permute-done.48
  296.0 3.1 collective-permute-done.43
  299.2 3.1 collective-permute-done.58
  305.5 3.1 collective-permute-done.49
  308.6 3.1 collective-permute-done.44
  316.4 6.7 %collective-permute-done.37 = bf16[48,1536]{1,0:T(8,128)(2,1)S(1)} collective-permute-done((bf16[48,1536]{1,0:T(8,128)(2,1)S(1)}, bf16[48,1536]{1,0:T(8,128)(2,1)S(1)}, u32[]{:S(2)}, u32[]{:S(2)}) %collective-permute-start.37) | collective-permute-done | bytes 147488 | tf_op jit(solution)/shard_map/ppermute | solution.py:113
  324.5 6.7 %collective-permute-done.38 = bf16[48,1536]{1,0:T(8,128)(2,1)S(1)} collective-permute-done((bf16[48,1536]{1,0:T(8,128)(2,1)S(1)}, bf16[48,1536]{1,0:T(8,128)(2,1)S(1)}, u32[]{:S(2)}, u32[]{:S(2)}) %collective-permute-start.38) | collective-permute-done | bytes 147488 | tf_op jit(solution)/shard_map/ppermute | solution.py:113
  332.6 5.6 %collective-permute-done.39 = bf16[48,1536]{1,0:T(8,128)(2,1)S(1)} collective-permute-done((bf16[48,1536]{1,0:T(8,128)(2,1)S(1)}, bf16[48,1536]{1,0:T(8,128)(2,1)S(1)}, u32[]{:S(2)}, u32[]{:S(2)}) %collective-permute-start.39) | collective-permute-done | bytes 147488 | tf_op jit(solution)/shard_map/ppermute | solution.py:113
  (314 shorter events, 129.5 us)
Async XLA Ops:
  3.7 16.4 %collective-permute-start.1 = (bf16[48,1536]{1,0:T(8,128)(2,1)}, bf16[48,1536]{1,0:T(8,128)(2,1)S(1)}, u32[]{:S(2)}, u32[]{:S(2)}) collective-permute-start(bf16[48,1536]{1,0:T(8,128)(2,1)} %get-tuple-element.80), channel_id=1, source_target_pairs={{0,8},{2,10},{4,12},{6,14},{8,16},{10,18},{12,20},{14,22},{16,24},... | collective-permute-start | bytes 442376 | tf_op jit(solution)/shard_map/ppermute | solution.py:113
  6.7 38.1 %collective-permute-start.4 = (bf16[48,1536]{1,0:T(8,128)(2,1)}, bf16[48,1536]{1,0:T(8,128)(2,1)}, u32[]{:S(2)}, u32[]{:S(2)}) collective-permute-start(bf16[48,1536]{1,0:T(8,128)(2,1)} %get-tuple-element.80), channel_id=1, source_target_pairs={{0,4},{2,6},{4,0},{6,2},{8,12},{10,14},{12,8},{14,10},{16,20},{18,... | collective-permute-start | bytes 442376 | tf_op jit(solution)/shard_map/ppermute | solution.py:113
  9.3 19.6 %collective-permute-start.10 = (bf16[48,3072]{1,0:T(8,128)(2,1)S(1)}, bf16[48,3072]{1,0:T(8,128)(2,1)}, u32[]{:S(2)}, u32[]{:S(2)}) collective-permute-start(bf16[48,3072]{1,0:T(8,128)(2,1)S(1)} %bitcast.56), channel_id=1, source_target_pairs={{0,8},{2,10},{4,12},{6,14},{8,16},{10,18},{12,20},{14,22},{16,24},... | collective-permute-start | bytes 884744 | tf_op jit(solution)/shard_map/ppermute | solution.py:113
  10.9 71.1 %collective-permute-start.13 = (bf16[48,3072]{1,0:T(8,128)(2,1)S(1)}, bf16[48,3072]{1,0:T(8,128)(2,1)}, u32[]{:S(2)}, u32[]{:S(2)}) collective-permute-start(bf16[48,3072]{1,0:T(8,128)(2,1)S(1)} %bitcast.57), channel_id=1, source_target_pairs={{0,4},{2,6},{4,0},{6,2},{8,12},{10,14},{12,8},{14,10},{16,20},{18,... | collective-permute-start | bytes 884744 | tf_op jit(solution)/shard_map/ppermute | solution.py:113
  11.5 25.9 %collective-permute-start.18 = (bf16[48,3072]{1,0:T(8,128)(2,1)S(1)}, bf16[48,3072]{1,0:T(8,128)(2,1)}, u32[]{:S(2)}, u32[]{:S(2)}) collective-permute-start(bf16[48,3072]{1,0:T(8,128)(2,1)S(1)} %bitcast.53), channel_id=1, source_target_pairs={{0,8},{2,10},{4,12},{6,14},{8,16},{10,18},{12,20},{14,22},{16,24},... | collective-permute-start | bytes 884744 | tf_op jit(solution)/shard_map/ppermute | solution.py:113
  26.1 78.5 %collective-permute-start.21 = (bf16[48,3072]{1,0:T(8,128)(2,1)S(1)}, bf16[48,3072]{1,0:T(8,128)(2,1)S(1)}, u32[]{:S(2)}, u32[]{:S(2)}) collective-permute-start(bf16[48,3072]{1,0:T(8,128)(2,1)S(1)} %bitcast.55), channel_id=1, source_target_pairs={{0,4},{2,6},{4,0},{6,2},{8,12},{10,14},{12,8},{14,10},{16,20},{18,... | collective-permute-start | bytes 884744 | tf_op jit(solution)/shard_map/ppermute | solution.py:113
  35.9 110.2 %collective-permute-start.27 = (bf16[144,768]{1,0:T(8,128)(2,1)S(1)}, bf16[144,768]{1,0:T(8,128)(2,1)S(1)}, u32[]{:S(2)}, u32[]{:S(2)}) collective-permute-start(bf16[144,768]{1,0:T(8,128)(2,1)S(1)} %copy-done.27), channel_id=1, source_target_pairs={{0,1},{1,0},{2,3},{3,2},{4,5},{5,4},{6,7},{7,6},{8,9},{9,8},{10,11... | collective-permute-start | bytes 663560 | tf_op jit(solution)/shard_map/ppermute | solution.py:189
  57.6 25.5 %collective-permute-start.14 = (bf16[48,3072]{1,0:T(8,128)(2,1)}, bf16[48,3072]{1,0:T(8,128)(2,1)S(1)}, u32[]{:S(2)}, u32[]{:S(2)}) collective-permute-start(bf16[48,3072]{1,0:T(8,128)(2,1)} %collective-permute-done.10), channel_id=1, source_target_pairs={{0,4},{2,6},{4,0},{6,2},{8,12},{10,14},{12,8},{14,10},{16,20},{18,... | collective-permute-start | bytes 884744 | tf_op jit(solution)/shard_map/ppermute | solution.py:113
  80.9 24.9 %collective-permute-start.22 = (bf16[48,3072]{1,0:T(8,128)(2,1)}, bf16[48,3072]{1,0:T(8,128)(2,1)S(1)}, u32[]{:S(2)}, u32[]{:S(2)}) collective-permute-start(bf16[48,3072]{1,0:T(8,128)(2,1)} %collective-permute-done.18), channel_id=1, source_target_pairs={{0,4},{2,6},{4,0},{6,2},{8,12},{10,14},{12,8},{14,10},{16,20},{18,... | collective-permute-start | bytes 884744 | tf_op jit(solution)/shard_map/ppermute | solution.py:113
  82.0 37.8 %collective-permute-start.8 = (bf16[384,1536]{1,0:T(8,128)(2,1)S(1)}, bf16[384,1536]{1,0:T(8,128)(2,1)S(1)}, u32[]{:S(2)}, u32[]{:S(2)}) collective-permute-start(bf16[384,1536]{1,0:T(8,128)(2,1)S(1)} %constant_dynamic-update-slice_fusion.2), channel_id=1, source_target_pairs={{0,2},{2,0},{4,6},{6,4},{8,10},{10,8},{12,14},{14,12},{16,18},{18,... | collective-permute-start | bytes 3538952 | tf_op jit(solution)/shard_map/ppermute | solution.py:113
  103.6 23.4 %collective-permute-start.23 = (bf16[48,3072]{1,0:T(8,128)(2,1)S(1)}, bf16[48,3072]{1,0:T(8,128)(2,1)S(1)}, u32[]{:S(2)}, u32[]{:S(2)}) collective-permute-start(bf16[48,3072]{1,0:T(8,128)(2,1)S(1)} %collective-permute-done.19), channel_id=1, source_target_pairs={{0,4},{2,6},{4,0},{6,2},{8,12},{10,14},{12,8},{14,10},{16,20},{18,... | collective-permute-start | bytes 884744 | tf_op jit(solution)/shard_map/ppermute | solution.py:113
  104.6 15.1 %collective-permute-start.16 = (bf16[48,3072]{1,0:T(8,128)(2,1)S(1)}, bf16[48,3072]{1,0:T(8,128)(2,1)S(1)}, u32[]{:S(2)}, u32[]{:S(2)}) collective-permute-start(bf16[48,3072]{1,0:T(8,128)(2,1)S(1)} %collective-permute-done.12), channel_id=1, source_target_pairs={{0,4},{2,6},{4,0},{6,2},{8,12},{10,14},{12,8},{14,10},{16,20},{18,... | collective-permute-start | bytes 884744 | tf_op jit(solution)/shard_map/ppermute | solution.py:113
  105.8 21.2 %collective-permute-start.24 = (bf16[48,3072]{1,0:T(8,128)(2,1)S(1)}, bf16[48,3072]{1,0:T(8,128)(2,1)S(1)}, u32[]{:S(2)}, u32[]{:S(2)}) collective-permute-start(bf16[48,3072]{1,0:T(8,128)(2,1)S(1)} %collective-permute-done.20), channel_id=1, source_target_pairs={{0,4},{2,6},{4,0},{6,2},{8,12},{10,14},{12,8},{14,10},{16,20},{18,... | collective-permute-start | bytes 884744 | tf_op jit(solution)/shard_map/ppermute | solution.py:113
  119.7 19.8 %collective-permute-start.17 = (bf16[384,3072]{1,0:T(8,128)(2,1)S(1)}, bf16[384,3072]{1,0:T(8,128)(2,1)S(1)}, u32[]{:S(2)}, u32[]{:S(2)}) collective-permute-start(bf16[384,3072]{1,0:T(8,128)(2,1)S(1)} %constant_dynamic-update-slice_fusion.11), channel_id=1, source_target_pairs={{0,2},{2,0},{4,6},{6,4},{8,10},{10,8},{12,14},{14,12},{16,18},{18,... | collective-permute-start | bytes 7077896 | tf_op jit(solution)/shard_map/ppermute | solution.py:113
  126.0 12.6 %collective-permute-start.9 = (bf16[288,768]{1,0:T(8,128)(2,1)S(1)}, bf16[288,768]{1,0:T(8,128)(2,1)S(1)}, u32[]{:S(2)}, u32[]{:S(2)}) collective-permute-start(bf16[288,768]{1,0:T(8,128)(2,1)S(1)} %pad_maximum_fusion.4), channel_id=1, source_target_pairs={{0,1},{1,0},{2,3},{3,2},{4,5},{5,4},{6,7},{7,6},{8,9},{9,8},{10,11... | collective-permute-start | bytes 1327112 | tf_op jit(solution)/shard_map/ppermute | solution.py:189
  127.1 15.9 %collective-permute-start.25 = (bf16[384,3072]{1,0:T(8,128)(2,1)S(1)}, bf16[384,3072]{1,0:T(8,128)(2,1)S(1)}, u32[]{:S(2)}, u32[]{:S(2)}) collective-permute-start(bf16[384,3072]{1,0:T(8,128)(2,1)S(1)} %constant_dynamic-update-slice_fusion.19), channel_id=1, source_target_pairs={{0,2},{2,0},{4,6},{6,4},{8,10},{10,8},{12,14},{14,12},{16,18},{18,... | collective-permute-start | bytes 7077896 | tf_op jit(solution)/shard_map/ppermute | solution.py:113
  176.1 51.2 %collective-permute-start.45 = (bf16[384,1536]{1,0:T(8,128)(2,1)}, bf16[384,1536]{1,0:T(8,128)(2,1)}, u32[]{:S(2)}, u32[]{:S(2)}) collective-permute-start(bf16[384,1536]{1,0:T(8,128)(2,1)} %convolution_convert_fusion.4), channel_id=1, source_target_pairs={{0,2},{2,0},{4,6},{6,4},{8,10},{10,8},{12,14},{14,12},{16,18},{18,... | collective-permute-start | bytes 3538952 | tf_op jit(solution)/shard_map/ppermute | solution.py:113
  176.1 53.5 %collective-permute-start.40 = (bf16[384,1536]{1,0:T(8,128)(2,1)}, bf16[384,1536]{1,0:T(8,128)(2,1)}, u32[]{:S(2)}, u32[]{:S(2)}) collective-permute-start(bf16[384,1536]{1,0:T(8,128)(2,1)} %convolution_convert_fusion.6), channel_id=1, source_target_pairs={{0,2},{2,0},{4,6},{6,4},{8,10},{10,8},{12,14},{14,12},{16,18},{18,... | collective-permute-start | bytes 3538952 | tf_op jit(solution)/shard_map/ppermute | solution.py:113
  176.6 55.5 %collective-permute-start.55 = (bf16[384,1536]{1,0:T(8,128)(2,1)}, bf16[384,1536]{1,0:T(8,128)(2,1)}, u32[]{:S(2)}, u32[]{:S(2)}) collective-permute-start(bf16[384,1536]{1,0:T(8,128)(2,1)} %convolution_convert_fusion), channel_id=1, source_target_pairs={{0,2},{2,0},{4,6},{6,4},{8,10},{10,8},{12,14},{14,12},{16,18},{18,... | collective-permute-start | bytes 3538952 | tf_op jit(solution)/shard_map/ppermute | solution.py:113
  176.7 57.6 %collective-permute-start.50 = (bf16[384,1536]{1,0:T(8,128)(2,1)}, bf16[384,1536]{1,0:T(8,128)(2,1)}, u32[]{:S(2)}, u32[]{:S(2)}) collective-permute-start(bf16[384,1536]{1,0:T(8,128)(2,1)} %convolution_convert_fusion.2), channel_id=1, source_target_pairs={{0,2},{2,0},{4,6},{6,4},{8,10},{10,8},{12,14},{14,12},{16,18},{18,... | collective-permute-start | bytes 3538952 | tf_op jit(solution)/shard_map/ppermute | solution.py:113
  228.7 16.2 %collective-permute-start.46 = (bf16[192,1536]{1,0:T(8,128)(2,1)S(1)}, bf16[192,1536]{1,0:T(8,128)(2,1)S(1)}, u32[]{:S(2)}, u32[]{:S(2)}) collective-permute-start(bf16[192,1536]{1,0:T(8,128)(2,1)S(1)} %add_convert_fusion.2), channel_id=1, source_target_pairs={{0,4},{2,6},{4,0},{6,2},{8,12},{10,14},{12,8},{14,10},{16,20},{18,... | collective-permute-start | bytes 1769480 | tf_op jit(solution)/shard_map/ppermute | solution.py:113
  230.9 26.7 %collective-permute-start.41 = (bf16[192,1536]{1,0:T(8,128)(2,1)S(1)}, bf16[192,1536]{1,0:T(8,128)(2,1)S(1)}, u32[]{:S(2)}, u32[]{:S(2)}) collective-permute-start(bf16[192,1536]{1,0:T(8,128)(2,1)S(1)} %add_convert_fusion.3), channel_id=1, source_target_pairs={{0,4},{2,6},{4,0},{6,2},{8,12},{10,14},{12,8},{14,10},{16,20},{18,... | collective-permute-start | bytes 1769480 | tf_op jit(solution)/shard_map/ppermute | solution.py:113
  233.3 36.9 %collective-permute-start.56 = (bf16[192,1536]{1,0:T(8,128)(2,1)S(1)}, bf16[192,1536]{1,0:T(8,128)(2,1)S(1)}, u32[]{:S(2)}, u32[]{:S(2)}) collective-permute-start(bf16[192,1536]{1,0:T(8,128)(2,1)S(1)} %add_convert_fusion), channel_id=1, source_target_pairs={{0,4},{2,6},{4,0},{6,2},{8,12},{10,14},{12,8},{14,10},{16,20},{18,... | collective-permute-start | bytes 1769480 | tf_op jit(solution)/shard_map/ppermute | solution.py:113
  235.4 47.4 %collective-permute-start.51 = (bf16[192,1536]{1,0:T(8,128)(2,1)S(1)}, bf16[192,1536]{1,0:T(8,128)(2,1)S(1)}, u32[]{:S(2)}, u32[]{:S(2)}) collective-permute-start(bf16[192,1536]{1,0:T(8,128)(2,1)S(1)} %add_convert_fusion.1), channel_id=1, source_target_pairs={{0,4},{2,6},{4,0},{6,2},{8,12},{10,14},{12,8},{14,10},{16,20},{18,... | collective-permute-start | bytes 1769480 | tf_op jit(solution)/shard_map/ppermute | solution.py:113
  237.9 76.9 %collective-permute-start.36 = (bf16[192,1536]{1,0:T(8,128)(2,1)S(1)}, bf16[192,1536]{1,0:T(8,128)(2,1)S(1)}, u32[]{:S(2)}, u32[]{:S(2)}) collective-permute-start(bf16[192,1536]{1,0:T(8,128)(2,1)S(1)} %add_convert_fusion.4), channel_id=1, source_target_pairs={{0,4},{2,6},{4,0},{6,2},{8,12},{10,14},{12,8},{14,10},{16,20},{18,... | collective-permute-start | bytes 1769480 | tf_op jit(solution)/shard_map/ppermute | solution.py:113
  246.2 38.0 %collective-permute-start.47 = (bf16[48,1536]{1,0:T(8,128)(2,1)S(1)}, bf16[48,1536]{1,0:T(8,128)(2,1)S(1)}, u32[]{:S(2)}, u32[]{:S(2)}) collective-permute-start(bf16[48,1536]{1,0:T(8,128)(2,1)S(1)} %slice.624), channel_id=1, source_target_pairs={{0,8},{2,10},{4,12},{6,14},{8,16},{10,18},{12,20},{14,22},{16,24},... | collective-permute-start | bytes 442376 | tf_op jit(solution)/shard_map/ppermute | solution.py:113
  258.9 26.6 %collective-permute-start.42 = (bf16[48,1536]{1,0:T(8,128)(2,1)S(1)}, bf16[48,1536]{1,0:T(8,128)(2,1)S(1)}, u32[]{:S(2)}, u32[]{:S(2)}) collective-permute-start(bf16[48,1536]{1,0:T(8,128)(2,1)S(1)} %slice.625), channel_id=1, source_target_pairs={{0,8},{2,10},{4,12},{6,14},{8,16},{10,18},{12,20},{14,22},{16,24},... | collective-permute-start | bytes 442376 | tf_op jit(solution)/shard_map/ppermute | solution.py:113
  271.5 14.1 %collective-permute-start.57 = (bf16[48,1536]{1,0:T(8,128)(2,1)S(1)}, bf16[48,1536]{1,0:T(8,128)(2,1)S(1)}, u32[]{:S(2)}, u32[]{:S(2)}) collective-permute-start(bf16[48,1536]{1,0:T(8,128)(2,1)S(1)} %slice.622), channel_id=1, source_target_pairs={{0,8},{2,10},{4,12},{6,14},{8,16},{10,18},{12,20},{14,22},{16,24},... | collective-permute-start | bytes 442376 | tf_op jit(solution)/shard_map/ppermute | solution.py:113
  285.5 13.6 %collective-permute-start.43 = (bf16[48,1536]{1,0:T(8,128)(2,1)S(1)}, bf16[48,1536]{1,0:T(8,128)(2,1)S(1)}, u32[]{:S(2)}, u32[]{:S(2)}) collective-permute-start(bf16[48,1536]{1,0:T(8,128)(2,1)S(1)} %fusion.100), channel_id=1, source_target_pairs={{0,8},{2,10},{4,12},{6,14},{8,16},{10,18},{12,20},{14,22},{16,24},... | collective-permute-start | bytes 442376 | tf_op jit(solution)/shard_map/ppermute | solution.py:113
  285.6 16.6 %collective-permute-start.58 = (bf16[48,1536]{1,0:T(8,128)(2,1)S(1)}, bf16[48,1536]{1,0:T(8,128)(2,1)S(1)}, u32[]{:S(2)}, u32[]{:S(2)}) collective-permute-start(bf16[48,1536]{1,0:T(8,128)(2,1)S(1)} %fusion.91), channel_id=1, source_target_pairs={{0,8},{2,10},{4,12},{6,14},{8,16},{10,18},{12,20},{14,22},{16,24},... | collective-permute-start | bytes 442376 | tf_op jit(solution)/shard_map/ppermute | solution.py:113
  292.8 12.6 %collective-permute-start.53 = (bf16[48,1536]{1,0:T(8,128)(2,1)S(1)}, bf16[48,1536]{1,0:T(8,128)(2,1)S(1)}, u32[]{:S(2)}, u32[]{:S(2)}) collective-permute-start(bf16[48,1536]{1,0:T(8,128)(2,1)S(1)} %fusion.94), channel_id=1, source_target_pairs={{0,8},{2,10},{4,12},{6,14},{8,16},{10,18},{12,20},{14,22},{16,24},... | collective-permute-start | bytes 442376 | tf_op jit(solution)/shard_map/ppermute | solution.py:113
  299.1 12.6 %collective-permute-start.44 = (bf16[48,1536]{1,0:T(8,128)(2,1)S(1)}, bf16[48,1536]{1,0:T(8,128)(2,1)S(1)}, u32[]{:S(2)}, u32[]{:S(2)}) collective-permute-start(bf16[48,1536]{1,0:T(8,128)(2,1)S(1)} %fusion.101), channel_id=1, source_target_pairs={{0,8},{2,10},{4,12},{6,14},{8,16},{10,18},{12,20},{14,22},{16,24},... | collective-permute-start | bytes 442376 | tf_op jit(solution)/shard_map/ppermute | solution.py:113
  (56 other events, 475.7 us)
